TPU v7x, 32 devices: a whole 2x2x4 slice. The times are simulated.
32 devices in a mesh: rep: 2 (over y), pool: 2 (over core), tp: 8 (over z, x).
Axes of the slice: x: 2, y: 2, z: 4, core: 2. Of those that a mesh axis runs over, the one named last changes fastest.
Arguments:
- hidden: bfloat16 [512, 16384], P(('rep', 'pool'), 'tp'), parts along dimension 0, may hold values from -6 to 6
- row_request_slots: int32 [512], P('rep'), parts along dimension 0, may hold values from 0 to 31
- requests: int32 [4, 32], P('rep'), parts along dimension 0, may hold values from 0 to 127
- adapter_page_table: int32 [128], replicated, may hold values from 0 to 127, each once
- down_matrix: bfloat16 [16384, 8192], P('tp'), may hold values from -0.046875 to 0.046875
- shrink_pool_pages: bfloat16 [128, 64, 16384], P('pool', None, 'tp'), may hold values from -0.046875 to 0.046875
- expand_pool_pages: bfloat16 [128, 64, 8192], P('pool', None, 'tp'), may hold values from -0.75 to 0.75
Outputs:
- projected: bfloat16 [512, 8192], P(('rep', 'pool'), 'tp'), parts along dimension 0
There are 2 independent parts, one for each index of `rep`. A program takes and returns all parts, laid end to end along the dimension named above; an argument that names none is the same for every part. Nothing has to cross between parts.
All inputs are finite; a program needn't handle non-finite values.
Results may differ from a plain program's by a relative error of at most 0.0039.
Values may be sent and summed in bfloat16 or wider, within the bound.
A program may use at most 256 MiB of HBM per device.

v0:
```python
import jax
import jax.numpy as jnp
from jax import lax
from jax.sharding import PartitionSpec as P


def owner_split(adapters, adapter_page_table, per_holder_count):
    page_numbers = jnp.take(adapter_page_table, adapters, axis=0)
    return (page_numbers // per_holder_count, page_numbers % per_holder_count)


def shrink_select(rows_in, pages_a, onehot_picker):
    scores = jnp.einsum("rf,pkf->rpk", rows_in, pages_a, preferred_element_type=jnp.float32)
    return jnp.sum(scores * onehot_picker[:, :, None], axis=1)


def expand_choice_mask(rank_activation, expand_page_rows, onehot_picker):
    weighted = (onehot_picker[:, :, None] * rank_activation.astype(jnp.float32)[:, None, :]).astype(
        jnp.bfloat16
    )
    flat_rows = weighted.reshape(weighted.shape[0], -1)
    flat_pages = expand_page_rows.reshape(-1, expand_page_rows.shape[2])
    return jnp.dot(flat_rows, flat_pages, preferred_element_type=jnp.float32)


def local(
    hidden,
    row_request_slots,
    requests,
    adapter_page_table,
    down_matrix,
    shrink_pool_pages,
    expand_pool_pages,
):
    rows_dev = hidden.shape[0]
    per_holder_count = shrink_pool_pages.shape[0]
    pool_index = lax.axis_index("pool")
    partial_value = jnp.dot(hidden, down_matrix, preferred_element_type=jnp.float32)
    base_output = lax.psum_scatter(partial_value, "tp", scatter_dimension=1, tiled=True)
    owner_index, shard_local_pages = owner_split(requests, adapter_page_table, per_holder_count)
    holder_slots = (owner_index == pool_index)[:, :, None, None]
    empty_filler = jnp.zeros((), jnp.bfloat16)
    sent_shrink_pages = jnp.where(
        holder_slots, jnp.take(shrink_pool_pages, shard_local_pages, axis=0), empty_filler
    )
    sent_expand_pages = jnp.where(
        holder_slots, jnp.take(expand_pool_pages, shard_local_pages, axis=0), empty_filler
    )
    fetched_a, fetched_b = (
        lax.all_to_all(sent_shrink_pages, "pool", split_axis=0, concat_axis=0, tiled=True),
        lax.all_to_all(sent_expand_pages, "pool", split_axis=0, concat_axis=0, tiled=True),
    )
    pages_a = jnp.sum(fetched_a, axis=0)
    expand_page_rows = jnp.sum(fetched_b, axis=0)
    own_slots = lax.dynamic_slice_in_dim(row_request_slots, pool_index * rows_dev, rows_dev, 0)
    slot_range = jnp.arange(pages_a.shape[0], dtype=jnp.int32)
    onehot_picker = (own_slots[:, None] == slot_range[None, :]).astype(jnp.float32)
    shrink_part = shrink_select(hidden, pages_a, onehot_picker)
    rank_activation = lax.psum(shrink_part, "tp").astype(jnp.bfloat16)
    adapter_update = expand_choice_mask(rank_activation, expand_page_rows, onehot_picker)
    return (base_output + adapter_update).astype(jnp.bfloat16)


def solution(mesh):
    return jax.shard_map(
        local,
        mesh=mesh,
        in_specs=(
            P(("rep", "pool"), "tp"),
            P("rep"),
            P("rep", None),
            P(),
            P("tp", None),
            P("pool", None, "tp"),
            P("pool", None, "tp"),
        ),
        out_specs=P(("rep", "pool"), "tp"),
        check_vma=False,
    )
```

profile of v0, /device:TPU:0, one launch (start us, length us, event | category | flops | bytes accessed | tf_op | source)
XLA Modules:
  0.0 166.6 jit_solution(11102554688308564500)
XLA Ops:
  6.5 0.0 copy-start
  6.5 0.0 copy-start.2
  6.5 0.0 copy-start.1
  6.5 0.0 reduce-scatter.2.cloned.1.call-start
  6.5 1.0 copy-done
  7.6 17.1 %fusion.9 = f32[128,8192]{1,0:T(8,128)} fusion(bf16[128,2048]{1,0:T(8,128)(2,1)S(1)} %copy-done, bf16[2048,8192]{1,0:T(8,128)(2,1)} %param.11), kind=kOutput, calls=%fused_computation.32 | convolution fusion | flops 4294967296 | bytes 38273024 | tf_op jit(solution)/shard_map/dot_general | solution.py:38
  24.7 0.0 reduce-scatter.2.cloned.1.call-update
  24.7 0.0 copy-done.2
  24.7 0.1 reshape.73
  24.8 0.0 copy-done.1
  24.8 0.8 gather_fusion
  25.6 0.1 reshape.72
  25.7 0.1 reshape.81
  25.8 13.4 %gather_fusion.1 = bf16[64,64,2048]{2,1,0:T(8,128)(2,1)} fusion(bf16[64,64,2048]{2,1,0:T(8,128)(2,1)} %param.12, s32[1024]{0:T(1024)S(1)} %pad_clamp_fusion), kind=kCustom, calls=%fused_computation.1 | custom fusion | bytes 33554688 | tf_op jit(solution)/shard_map/jit(_take)/gather | solution.py:44
  39.2 14.4 %select_select_fusion = bf16[2,32,64,2048]{3,2,1,0:T(8,128)(2,1)} fusion(bf16[2,32,64,2048]{3,2,1,0:T(8,128)(2,1)} %bitcast.21, pred[2,32]{1,0:T(4,128)(4,1)S(1)} %get-tuple-element.5, pred[2,32]{1,0:T(4,128)(4,1)S(1)} %get-tuple-element.7), kind=kLoop, calls=%fused_computation.3 | loop fusion | flops 16777216 | bytes 33554560 | tf_op jit(solution)/shard_map/jit(_where)/select_n | solution.py:43
  53.6 9.7 %all-to-all-start = ((bf16[2,32,64,2048]{3,2,1,0:T(8,128)(2,1)}), bf16[2,32,64,2048]{3,2,1,0:T(8,128)(2,1)}, u32[]{:S(2)}, u32[]{:S(2)}) async-start(bf16[2,32,64,2048]{3,2,1,0:T(8,128)(2,1)} %select_select_fusion), calls=%async_computation.1 | async-start | bytes 33554432 | tf_op jit(solution)/shard_map/all_to_all | solution.py:50
  63.4 0.0 copy-start.3
  63.4 9.1 %gather_fusion.2 = bf16[64,64,1024]{2,1,0:T(8,128)(2,1)} fusion(bf16[64,64,1024]{2,1,0:T(8,128)(2,1)} %param.13, s32[1024]{0:T(1024)S(1)} %pad_clamp_fusion), kind=kCustom, calls=%fused_computation.2 | custom fusion | bytes 16777472 | tf_op jit(solution)/shard_map/jit(_take)/gather | solution.py:47
  72.5 0.0 copy-done.3
  72.5 0.1 dynamic_slice.3
  72.6 7.6 %select_select_fusion.1 = bf16[2,32,64,1024]{3,2,1,0:T(8,128)(2,1)} fusion(bf16[2,32,64,1024]{3,2,1,0:T(8,128)(2,1)} %bitcast.22, pred[2,32]{1,0:T(4,128)(4,1)S(1)} %get-tuple-element.5, pred[2,32]{1,0:T(4,128)(4,1)S(1)} %get-tuple-element.7), kind=kLoop, calls=%fused_computation.4 | loop fusion | flops 8388608 | bytes 16777344 | tf_op jit(solution)/shard_map/jit(_where)/select_n | solution.py:46
  80.2 0.0 all-to-all-done
  80.2 7.1 %all-to-all-start.1 = ((bf16[2,32,64,1024]{3,2,1,0:T(8,128)(2,1)}), bf16[2,32,64,1024]{3,2,1,0:T(8,128)(2,1)}, u32[]{:S(2)}, u32[]{:S(2)}) async-start(bf16[2,32,64,1024]{3,2,1,0:T(8,128)(2,1)} %select_select_fusion.1), calls=%async_computation.2 | async-start | bytes 16777216 | tf_op jit(solution)/shard_map/all_to_all | solution.py:51
  87.3 14.7 %reduce_sum.33 = bf16[32,64,2048]{2,1,0:T(8,128)(2,1)} reduce(bf16[2,32,64,2048]{3,2,1,0:T(8,128)(2,1)} %all-to-all-done, bf16[]{:T(256)} %constant.84.clone.1), dimensions={0}, to_apply=%region_1.2 | reduce | flops 4194304 | bytes 25165826 | tf_op jit(solution)/shard_map/reduce_sum | solution.py:53
  102.0 5.8 %fusion.1 = f32[128,64]{0,1:T(8,128)S(1)} fusion(bf16[32,64,2048]{2,1,0:T(8,128)(2,1)} %reduce_sum.33, bf16[128,2048]{1,0:T(8,128)(2,1)S(1)} %copy-done, f32[128,32]{0,1:T(8,128)S(1)} %fusion.7), kind=kOutput, calls=%fused_computation.7 | convolution fusion | flops 1074257920 | bytes 8962048 | tf_op jit(solution)/shard_map/rf,pkf->rpk/dot_general | solution.py:13
  107.8 39.2 %psum.7 = bf16[128,64]{0,1:T(8,128)(2,1)S(1)} all-reduce(f32[128,64]{0,1:T(8,128)S(1)} %fusion.1), channel_id=1, replica_groups=mesh['rep'=2,'pool'=2,'tp'=8] {'tp'}, use_global_device_ids=true, to_apply=%region_3.4 | all-reduce | flops 8192 | bytes 49152 | tf_op jit(solution)/shard_map/psum | solution.py:59
  147.0 0.0 all-to-all-done.1
  147.0 9.0 %reduce_sum.35 = bf16[32,64,1024]{2,1,0:T(8,128)(2,1)} reduce(bf16[2,32,64,1024]{3,2,1,0:T(8,128)(2,1)} %all-to-all-done.1, bf16[]{:T(256)} %constant.84.clone.1), dimensions={0}, to_apply=%region_4.5 | reduce | flops 2097152 | bytes 12582914 | tf_op jit(solution)/shard_map/reduce_sum | solution.py:54
  156.0 0.0 reduce-scatter.2.cloned.1.call-done
  156.0 3.8 %fusion.3 = bf16[128,1024]{1,0:T(8,128)(2,1)} fusion(f32[128,1024]{1,0:T(8,128)} %reduce-scatter.2.cloned.1.call-done, bf16[32,64,1024]{2,1,0:T(8,128)(2,1)} %reduce_sum.35, f32[128,64]{0,1:T(8,128)S(1)} %convert_element_type.34, f32[128,32]{0,1:T(8,128)S(1)} %fusion.7), kind=kOutput, calls=%fused_computation.10 | convolution fusion | flops 537657344 | bytes 5029888 | tf_op jit(solution)/shard_map/dot_general | solution.py:23
  (6 shorter events, 0.1 us)
Async XLA Ops:
  6.5 1.0 copy-start
  6.5 18.2 %copy-start.2 = (s32[2,32]{1,0:T(2,128)S(1)}, s32[2,32]{1,0:T(2,128)}, u32[]{:S(2)}) copy-start(s32[2,32]{1,0:T(2,128)} %param.9) | copy-start | bytes 772
  6.5 18.3 %copy-start.1 = (s32[128]{0:T(128)S(1)}, s32[128]{0:T(128)}, u32[]{:S(2)}) copy-start(s32[128]{0:T(128)} %param.10) | copy-start | bytes 1540
  6.5 149.5 %reduce-scatter.2.cloned.1.call-start = ((), (), s32[]{:S(2)}) async-start(), calls=%async_computation.3 | async-start | bytes 4718592 | tf_op jit(solution)/shard_map/reduce_scatter | solution.py:39
  53.6 26.6 %all-to-all-start = ((bf16[2,32,64,2048]{3,2,1,0:T(8,128)(2,1)}), bf16[2,32,64,2048]{3,2,1,0:T(8,128)(2,1)}, u32[]{:S(2)}, u32[]{:S(2)}) async-start(bf16[2,32,64,2048]{3,2,1,0:T(8,128)(2,1)} %select_select_fusion), calls=%async_computation.1 | async-start | bytes 33554432 | tf_op jit(solution)/shard_map/all_to_all | solution.py:50
  63.4 9.1 %copy-start.3 = (s32[256]{0:T(256)S(1)}, s32[256]{0:T(256)}, u32[]{:S(2)}) copy-start(s32[256]{0:T(256)} %param.8) | copy-start | bytes 3076
  80.2 66.8 %all-to-all-start.1 = ((bf16[2,32,64,1024]{3,2,1,0:T(8,128)(2,1)}), bf16[2,32,64,1024]{3,2,1,0:T(8,128)(2,1)}, u32[]{:S(2)}, u32[]{:S(2)}) async-start(bf16[2,32,64,1024]{3,2,1,0:T(8,128)(2,1)} %select_select_fusion.1), calls=%async_computation.2 | async-start | bytes 16777216 | tf_op jit(solution)/shard_map/all_to_all | solution.py:51
Sparse Core Ops, SparseCore 0:
  24.8 91.0 reduce-scatter.1
where the time goes:
time: 167 us
  other arithmetic  45.8 us (27%)
  blocking collectives  39.2 us (23%)
  matrix products  26.6 us (16%)
  local copies, waits for them, and re-layouts  24.6 us (15%)
  starting transfers between devices  16.9 us (10%)
  between operations  13.5 us (8%)
    psum x1, blocking collectives, local(): rank_activation = lax.psum(shrink_part, 'tp').astype(jnp.bfloat16)  39.2 us
    dot_general x1, matrix products, local(): jnp.dot(hidden, down_matrix, preferred_element_type=jnp.float32)  17.1 us
    reduce_sum x1, other arithmetic, local(): pages_a = jnp.sum(fetched_a, axis=0)  14.7 us
    select_n x1, other arithmetic, local(): jnp.where(holder_slots, jnp.take(shrink_pool_pages, shard_local_pages, ax...  14.4 us
    gather x1, local copies, waits for them, and re-layouts, local(): jnp.take(shrink_pool_pages, shard_local_pages, axis=0)  13.4 us
    all_to_all x1, starting transfers between devices, local(): lax.all_to_all(sent_shrink_pages, 'pool', split_axis=0, concat_axis=0, ti...  9.75 us
    gather x1, local copies, waits for them, and re-layouts, local(): jnp.take(expand_pool_pages, shard_local_pages, axis=0)  9.12 us
    reduce_sum x1, other arithmetic, local(): expand_page_rows = jnp.sum(fetched_b, axis=0)  9.02 us
  transfers between devices with their start and end apart: 3, of which 0 were waited for; matrix products, arithmetic and copies ran while one was open for 45% of the time, Pallas kernels for 0%

commit v1 on v0

--- a/solution.py
+++ b/solution.py
@@ -1,7 +1,14 @@
+import functools
+
 import jax
 import jax.numpy as jnp
 from jax import lax
+from jax.experimental import pallas as pl
+from jax.experimental.pallas import tpu as pltpu
 from jax.sharding import PartitionSpec as P
+
+MESH = pl.DeviceIdType.MESH
+DEPTH = 6
 
 
 def owner_split(adapters, adapter_page_table, per_holder_count):
@@ -23,7 +30,7 @@
     return jnp.dot(flat_rows, flat_pages, preferred_element_type=jnp.float32)
 
 
-def local(
+def local_general(
     hidden,
     row_request_slots,
     requests,
@@ -61,9 +68,339 @@
     return (base_output + adapter_update).astype(jnp.bfloat16)
 
 
+def fused_kernel(
+    slots_ref,
+    requests_ref,
+    table_ref,
+    hidden_ref,
+    down_ref,
+    shrink_ref,
+    expand_ref,
+    out_ref,
+    hid,
+    wbuf,
+    sbuf,
+    ebuf,
+    own,
+    xs,
+    xr,
+    zs,
+    zr,
+    bs,
+    br,
+    delta,
+    ds_,
+    dr,
+    pack,
+    lrr,
+    lrs,
+    lrg,
+    load_sem,
+    hid_sem,
+    x_sem,
+    z_sem,
+    b_sem,
+    d_sem,
+    l_sem,
+    g_sem,
+):
+    rep = lax.axis_index("rep")
+    c = lax.axis_index("pool")
+    tp = lax.axis_index("tp")
+    z, x = tp // 2, tp % 2
+    rows = hidden_ref.shape[0]
+    half = out_ref.shape[1] // 2
+    lane = lambda shape: lax.broadcasted_iota(jnp.int32, shape, 1)
+
+    def dev(pool, t):
+        return (rep, pool, t)
+
+    zdest = [(z + 2) % 4, 3 - z, z + 1 - 2 * (z % 2), z]
+
+    def column(zz, xx):
+        return pl.multiple_of((zz * 2 + xx) * (2 * half) + c * half, half)
+
+    def down_load(slot, zz, xx):
+        return down_ref.at[:, pl.ds(column(zz, xx), half)], wbuf.at[slot]
+
+    loads = []
+    keys = {}
+
+    def add(key, pair):
+        k = len(loads)
+        keys[key] = k
+        loads.append(pltpu.make_async_copy(pair[0], pair[1], load_sem.at[k]))
+
+    for i in (0, 1):
+        add(("r", i), down_load(i, zdest[i], 1 - x))
+    for i in (0, 1):
+        add(("o", i), down_load(4 + i, zdest[i], x))
+    for i in range(8):
+        add(("s", i), (shrink_ref.at[pl.ds(i * 512, 512), :], sbuf.at[i]))
+    for i in (2, 3):
+        add(("r", i), down_load(i, zdest[i], 1 - x))
+    for i in (2, 3):
+        add(("o", i), down_load(4 + i, zdest[i], x))
+    for i in range(4):
+        add(("e", i), (expand_ref.at[pl.ds(i * 1024, 1024), :], ebuf.at[i]))
+
+    mine = pl.ds(pl.multiple_of(c * rows, rows), rows)
+    theirs = pl.ds(pl.multiple_of((1 - c) * rows, rows), rows)
+    hid_local = pltpu.make_async_copy(hidden_ref, hid.at[mine], hid_sem.at[2])
+    hid_local.start()
+    for k in range(DEPTH):
+        loads[k].start()
+
+    def use(key):
+        k = keys[key]
+        loads[k].wait()
+        if k + DEPTH < len(loads):
+            loads[k + DEPTH].start()
+
+    barrier = pltpu.get_barrier_semaphore()
+    for step in range(1, 8):
+        pl.semaphore_signal(barrier, inc=1, device_id=dev(c, (tp + step) % 8), device_id_type=MESH)
+    for zz in zdest:
+        pl.semaphore_signal(barrier, inc=1, device_id=dev(1 - c, zz * 2 + x), device_id_type=MESH)
+    pl.semaphore_wait(barrier, 11)
+
+    hid_swap = pltpu.make_async_remote_copy(
+        src_ref=hidden_ref, dst_ref=hid.at[mine],
+        send_sem=hid_sem.at[0], recv_sem=hid_sem.at[1],
+        device_id=dev(1 - c, tp), device_id_type=MESH,
+    )
+    hid_swap.start()
+
+    first_shard = lax.broadcasted_iota(jnp.int32, (2 * rows, 32), 0) < rows
+    entry = jnp.where(first_shard, requests_ref[0:1, :], requests_ref[1:2, :])
+    adapter = jnp.sum(
+        jnp.where(lane((2 * rows, 32)) == slots_ref[...], entry, 0), axis=1, keepdims=True
+    )
+    page = jnp.sum(
+        jnp.where(lane((2 * rows, 128)) == adapter, table_ref[...], 0), axis=1, keepdims=True
+    )
+    pid = page - c * 64
+    pid2 = jnp.broadcast_to(pid, (2 * rows, 128)) - lane((2 * rows, 128)) // 64
+
+    hid_local.wait()
+    hid_swap.wait()
+
+    xn = z * 2 + 1 - x
+    x_copies = {}
+
+    def remote_piece(i):
+        use(("r", i))
+        xs[i] = jnp.dot(hid[...], wbuf[i], preferred_element_type=jnp.float32).astype(jnp.bfloat16)
+        for h in range(2):
+            part = pl.ds(h * rows, rows)
+            x_copies[i, h] = pltpu.make_async_remote_copy(
+                src_ref=xs.at[i, part], dst_ref=xr.at[i, part],
+                send_sem=x_sem.at[0, 2 * i + h], recv_sem=x_sem.at[1, 2 * i + h],
+                device_id=dev(c, xn), device_id_type=MESH,
+            )
+            x_copies[i, h].start()
+
+    def own_piece(i):
+        use(("o", i))
+        own[i] = jnp.dot(hid[...], wbuf[4 + i], preferred_element_type=jnp.float32)
+
+    z_sends = []
+
+    def forward(i):
+        for h in range(2):
+            x_copies[i, h].wait_recv()
+            part = pl.ds(h * rows, rows)
+            zs[i, part] = (own[i, part] + xr[i, part].astype(jnp.float32)).astype(jnp.bfloat16)
+            copy = pltpu.make_async_remote_copy(
+                src_ref=zs.at[i, part], dst_ref=zr.at[i, c],
+                send_sem=z_sem.at[0, i, h], recv_sem=z_sem.at[1, i, c],
+                device_id=dev(h, zdest[i] * 2 + x), device_id_type=MESH,
+            )
+            copy.start()
+            z_sends.append(copy)
+
+    remote_piece(0)
+    remote_piece(1)
+    own_piece(0)
+    own_piece(1)
+
+    acc = jnp.zeros((2 * rows, 128), jnp.float32)
+    for i in range(8):
+        use(("s", i))
+        scores = lax.dot_general(
+            hid[...], sbuf[i], (((1,), (1,)), ((), ())), preferred_element_type=jnp.float32
+        )
+        for j in range(4):
+            acc = acc + jnp.where(pid2 == 8 * i + 2 * j, scores[:, j * 128 : j * 128 + 128], 0.0)
+    acc = acc + pltpu.roll(acc, 64, 1)
+    low = lane((rows, 128)) < 64
+    pack[...] = jnp.where(low, acc[:rows], acc[rows:])
+
+    l_copies = []
+    for step in range(1, 8):
+        to = (tp + step) % 8
+        copy = pltpu.make_async_remote_copy(
+            src_ref=pack.at[pl.ds(pl.multiple_of(to * 16, 16), 16)], dst_ref=lrr.at[step - 1],
+            send_sem=l_sem.at[0, step - 1], recv_sem=l_sem.at[1, step - 1],
+            device_id=dev(c, to), device_id_type=MESH,
+        )
+        copy.start()
+        l_copies.append(copy)
+
+    forward(0)
+    remote_piece(2)
+    remote_piece(3)
+    own_piece(2)
+    own_piece(3)
+    forward(1)
+
+    block = pl.ds(pl.multiple_of(tp * 16, 16), 16)
+    total = pack[block, :]
+    for step in range(1, 8):
+        l_copies[step - 1].wait_recv()
+        total = total + lrr[step - 1]
+    lrs[...] = total.astype(jnp.bfloat16)
+    lrg[block, :] = lrs[...]
+    g_copies = []
+    for step in range(1, 8):
+        to = (tp + step) % 8
+        copy = pltpu.make_async_remote_copy(
+            src_ref=lrs, dst_ref=lrg.at[block],
+            send_sem=g_sem.at[0, step - 1], recv_sem=g_sem.at[1, step - 1],
+            device_id=dev(c, to), device_id_type=MESH,
+        )
+        copy.start()
+        g_copies.append(copy)
+
+    forward(2)
+
+    for step in range(1, 8):
+        g_copies[step - 1].wait_recv()
+    packed = lrg[...].astype(jnp.float32)
+    turned = pltpu.roll(packed, 64, 1)
+    rank2 = jnp.concatenate(
+        [jnp.where(low, packed, turned), jnp.where(low, turned, packed)], axis=0
+    )
+    for i in range(4):
+        use(("e", i))
+        weighted = jnp.concatenate(
+            [
+                jnp.where(pid2 == 16 * i + 2 * j, rank2, 0.0).astype(jnp.bfloat16)
+                for j in range(8)
+            ],
+            axis=1,
+        )
+        part = jnp.dot(weighted, ebuf[i], preferred_element_type=jnp.float32)
+        if i == 0:
+            delta[...] = part
+        else:
+            delta[...] += part
+    ds_[...] = delta[theirs, :]
+    d_copy = pltpu.make_async_remote_copy(
+        src_ref=ds_, dst_ref=dr, send_sem=d_sem.at[0], recv_sem=d_sem.at[1],
+        device_id=dev(1 - c, tp), device_id_type=MESH,
+    )
+    d_copy.start()
+
+    for h in range(2):
+        x_copies[3, h].wait_recv()
+    bs[...] = own[3, theirs, :] + xr[3, theirs, :].astype(jnp.float32)
+    b_copy = pltpu.make_async_remote_copy(
+        src_ref=bs, dst_ref=br, send_sem=b_sem.at[0], recv_sem=b_sem.at[1],
+        device_id=dev(1 - c, tp), device_id_type=MESH,
+    )
+    b_copy.start()
+    own_cols = pl.ds(pl.multiple_of(c * half, half), half)
+    other_cols = pl.ds(pl.multiple_of((1 - c) * half, half), half)
+    base_own = own[3, mine, :] + xr[3, mine, :].astype(jnp.float32)
+    d_copy.wait_recv()
+    base_own = base_own + delta[mine, own_cols] + dr[:, own_cols]
+    b_copy.wait_recv()
+    base_other = br[...] + delta[mine, other_cols] + dr[:, other_cols]
+    for i in range(3):
+        for k in range(2):
+            pltpu.make_async_remote_copy(
+                src_ref=zr.at[i, k], dst_ref=zr.at[i, k],
+                send_sem=z_sem.at[0, i, k], recv_sem=z_sem.at[1, i, k],
+                device_id=dev(1 - c, tp), device_id_type=MESH,
+            ).wait_recv()
+        base_own = base_own + zr[i, c].astype(jnp.float32)
+        base_other = base_other + zr[i, 1 - c].astype(jnp.float32)
+    out_ref[:, own_cols] = base_own.astype(jnp.bfloat16)
+    out_ref[:, other_cols] = base_other.astype(jnp.bfloat16)
+
+    for copy in [*x_copies.values(), *z_sends, *l_copies, *g_copies, d_copy, b_copy]:
+        copy.wait_send()
+
+
+def local_fused(
+    hidden,
+    row_request_slots,
+    requests,
+    adapter_page_table,
+    down_matrix,
+    shrink_pool_pages,
+    expand_pool_pages,
+):
+    rows, depth = hidden.shape
+    pages, rank, width = expand_pool_pages.shape
+    half = width // 2
+    bf16, f32 = jnp.bfloat16, jnp.float32
+    vmem = pl.BlockSpec(memory_space=pltpu.VMEM)
+    hbm = pl.BlockSpec(memory_space=pl.ANY)
+    V = pltpu.VMEM
+    dma = pltpu.SemaphoreType.DMA
+    flat = pages * rank
+    return pl.pallas_call(
+        fused_kernel,
+        out_shape=jax.ShapeDtypeStruct((rows, width), bf16),
+        in_specs=[vmem, vmem, vmem, hbm, hbm, hbm, hbm],
+        out_specs=vmem,
+        scratch_shapes=[
+            V((2 * rows, depth), bf16),
+            V((8, depth, half), bf16),
+            V((8, flat // 8, depth), bf16),
+            V((4, flat // 4, width), bf16),
+            V((4, 2 * rows, half), f32),
+            V((4, 2 * rows, half), bf16),
+            V((4, 2 * rows, half), bf16),
+            V((3, 2 * rows, half), bf16),
+            V((3, 2, rows, half), bf16),
+            V((rows, half), f32),
+            V((rows, half), f32),
+            V((2 * rows, width), f32),
+            V((rows, width), f32),
+            V((rows, width), f32),
+            V((rows, 128), f32),
+            V((7, 16, 128), f32),
+            V((16, 128), bf16),
+            V((rows, 128), bf16),
+            dma((20,)),
+            dma((3,)),
+            dma((2, 8)),
+            dma((2, 3, 2)),
+            dma((2,)),
+            dma((2,)),
+            dma((2, 7)),
+            dma((2, 7)),
+        ],
+        compiler_params=pltpu.CompilerParams(
+            collective_id=0, has_side_effects=True, vmem_limit_bytes=60 * 1024 * 1024
+        ),
+    )(
+        row_request_slots.reshape(-1, 1),
+        requests,
+        adapter_page_table.reshape(1, -1),
+        hidden,
+        down_matrix,
+        shrink_pool_pages.reshape(flat, depth),
+        expand_pool_pages.reshape(flat, width),
+    )
+
+
 def solution(mesh):
     return jax.shard_map(
-        local,
+        local_fused if mesh.shape["tp"] == 8 else local_general,
         mesh=mesh,
         in_specs=(
             P(("rep", "pool"), "tp"),

time: 167 us -> 54.3 us (0.33)
  Pallas kernels: 0 us -> 50.8 us
  other arithmetic: 45.8 us -> 0 us
  blocking collectives: 39.2 us -> 0 us
  matrix products: 26.6 us -> 0 us
  local copies, waits for them, and re-layouts: 24.6 us -> 3.14 us
  starting transfers between devices: 16.9 us -> 0 us
  between operations: 13.5 us -> 0.01 us
    pallas_call x0 -> x1, Pallas kernels: none -> 50.8 us  [local_fused(): pl.pallas_call(fused_kernel, out_shape=jax.ShapeDtypeStruct((rows, width)...]
    psum x1 -> x0, blocking collectives: 39.2 us -> none  [local(): rank_activation = lax.psum(shrink_part, 'tp').astype(jnp.bfloat16)]
    dot_general x3 -> x0, matrix products: 26.6 us -> none  [the longest x1 17.1 us: local(): jnp.dot(hidden, down_matrix, preferred_element_type=jnp.float32)]
    reduce_sum x2 -> x0, other arithmetic: 23.8 us -> none  [the longest x1 14.7 us: local(): pages_a = jnp.sum(fetched_a, axis=0)]
    gather x4 -> x0, local copies, waits for them, and re-layouts: 23.3 us -> none  [the longest x1 13.4 us: local(): jnp.take(shrink_pool_pages, shard_local_pages, axis=0)]
    select_n x3 -> x0, other arithmetic: 22 us -> none  [the longest x1 14.4 us: local(): jnp.where(holder_slots, jnp.take(shrink_pool_pages, shard_local_pages, ax...]
    all_to_all x2 -> x0, starting transfers between devices: 16.9 us -> none  [the longest x1 9.75 us: local(): lax.all_to_all(sent_shrink_pages, 'pool', split_axis=0, concat_axis=0, ti...]
  transfers between devices with their start and end apart: 3 -> 0, of which waited for: 0 -> 0; matrix products, arithmetic and copies ran while one was open for 45% -> 0% of each run, Pallas kernels for 0% -> 0%
where the time goes in v1:
time: 54.3 us; the launch traced here: 53.9 us
  Pallas kernels  50.8 us (94%)
  local copies, waits for them, and re-layouts  3.14 us (6%)
    pallas_call x1, Pallas kernels, local_fused(): pl.pallas_call(fused_kernel, out_shape=jax.ShapeDtypeStruct((rows, width)...  50.8 us
    unnamed x1, local copies, waits for them, and re-layouts  1.67 us
    reshape x1, local copies, waits for them, and re-layouts, local_fused(): row_request_slots.reshape(-1, 1)  1.47 us

profile of v1, /device:TPU:0, one launch (start us, length us, event | category | flops | bytes accessed | tf_op | source)
XLA Modules:
  0.0 53.9 jit_solution(5245960772042427061)
XLA Ops:
  0.0 1.5 %copy.8.slots_ref = s32[256,1]{1,0:T(8,128)} copy(s32[256,1]{0,1:T(1,128)} %bitcast.6) | data formatting | bytes 2048 | tf_op jit(solution)/shard_map/reshape | solution.py:391
  1.5 50.8 %shard_map.73 = bf16[128,1024]{1,0:T(8,128)(2,1)} custom-call(s32[256,1]{1,0:T(8,128)} %copy.8.slots_ref, s32[2,32]{1,0:T(2,128)} %requests_ref.1, s32[1,128]{1,0:T(1,128)} %bitcast.7, bf16[128,2048]{1,0:T(8,128)(2,1)} %hidden_ref.1, bf16[2048,8192]{1,0:T(8,128)(2,1)} %down_ref.1, bf16[4096,2048]{1,0:T(8,128)(2,1)} %bitcast.4, bf16[4096,1024]{1,0:T(8,128)(2,1)} %bitcast.5), custom_call_target="tpu_custom_call" | custom-call | tf_op jit(solution)/shard_map/pallas_call | solution.py:354
  52.2 1.7 %copy.10 = bf16[128,1024]{1,0:T(8,128)(2,1)} copy(bf16[128,1024]{1,0:T(8,128)(2,1)} %shard_map.73) | data formatting | bytes 524288

commit v2 on v1

v2 whole, which is shorter than its diff:
```python
import functools

import jax
import jax.numpy as jnp
from jax import lax
from jax.experimental import pallas as pl
from jax.experimental.pallas import tpu as pltpu
from jax.sharding import PartitionSpec as P

MESH = pl.DeviceIdType.MESH
DEPTH = 6
SPLIT = 3


def owner_split(adapters, adapter_page_table, per_holder_count):
    page_numbers = jnp.take(adapter_page_table, adapters, axis=0)
    return (page_numbers // per_holder_count, page_numbers % per_holder_count)


def shrink_select(rows_in, pages_a, onehot_picker):
    scores = jnp.einsum("rf,pkf->rpk", rows_in, pages_a, preferred_element_type=jnp.float32)
    return jnp.sum(scores * onehot_picker[:, :, None], axis=1)


def expand_choice_mask(rank_activation, expand_page_rows, onehot_picker):
    weighted = (onehot_picker[:, :, None] * rank_activation.astype(jnp.float32)[:, None, :]).astype(
        jnp.bfloat16
    )
    flat_rows = weighted.reshape(weighted.shape[0], -1)
    flat_pages = expand_page_rows.reshape(-1, expand_page_rows.shape[2])
    return jnp.dot(flat_rows, flat_pages, preferred_element_type=jnp.float32)


def local_general(
    hidden,
    row_request_slots,
    requests,
    adapter_page_table,
    down_matrix,
    shrink_pool_pages,
    expand_pool_pages,
):
    rows_dev = hidden.shape[0]
    per_holder_count = shrink_pool_pages.shape[0]
    pool_index = lax.axis_index("pool")
    partial_value = jnp.dot(hidden, down_matrix, preferred_element_type=jnp.float32)
    base_output = lax.psum_scatter(partial_value, "tp", scatter_dimension=1, tiled=True)
    owner_index, shard_local_pages = owner_split(requests, adapter_page_table, per_holder_count)
    holder_slots = (owner_index == pool_index)[:, :, None, None]
    empty_filler = jnp.zeros((), jnp.bfloat16)
    sent_shrink_pages = jnp.where(
        holder_slots, jnp.take(shrink_pool_pages, shard_local_pages, axis=0), empty_filler
    )
    sent_expand_pages = jnp.where(
        holder_slots, jnp.take(expand_pool_pages, shard_local_pages, axis=0), empty_filler
    )
    fetched_a, fetched_b = (
        lax.all_to_all(sent_shrink_pages, "pool", split_axis=0, concat_axis=0, tiled=True),
        lax.all_to_all(sent_expand_pages, "pool", split_axis=0, concat_axis=0, tiled=True),
    )
    pages_a = jnp.sum(fetched_a, axis=0)
    expand_page_rows = jnp.sum(fetched_b, axis=0)
    own_slots = lax.dynamic_slice_in_dim(row_request_slots, pool_index * rows_dev, rows_dev, 0)
    slot_range = jnp.arange(pages_a.shape[0], dtype=jnp.int32)
    onehot_picker = (own_slots[:, None] == slot_range[None, :]).astype(jnp.float32)
    shrink_part = shrink_select(hidden, pages_a, onehot_picker)
    rank_activation = lax.psum(shrink_part, "tp").astype(jnp.bfloat16)
    adapter_update = expand_choice_mask(rank_activation, expand_page_rows, onehot_picker)
    return (base_output + adapter_update).astype(jnp.bfloat16)


def fused_kernel(
    slots_ref,
    requests_ref,
    table_ref,
    hidden_ref,
    down_ref,
    shrink_ref,
    expand_ref,
    out_ref,
    hid,
    wbuf,
    sbuf,
    ebuf,
    own,
    xs,
    xr,
    zs,
    pair,
    last,
    bs,
    br,
    delta,
    ds_,
    dr,
    pack,
    lrr,
    lrs,
    lrg,
    load_sem,
    hid_sem,
    x_sem,
    z_sem,
    b_sem,
    d_sem,
    l_sem,
    g_sem,
):
    rep = lax.axis_index("rep")
    c = lax.axis_index("pool")
    tp = lax.axis_index("tp")
    z, x = tp // 2, tp % 2
    rows = hidden_ref.shape[0]
    half = out_ref.shape[1] // 2
    f32, bf16 = jnp.float32, jnp.bfloat16
    lane = lambda shape: lax.broadcasted_iota(jnp.int32, shape, 1)

    def dev(pool, t):
        return (rep, pool, t)

    near, far = z + 1 - 2 * (z % 2), (z + 2) % 4
    zdest = [3 - z, far, near, z]

    def column(zz, xx):
        return pl.multiple_of((zz * 2 + xx) * (2 * half) + c * half, half)

    loads = []
    keys = {}

    def add(key, source, target):
        k = len(loads)
        keys[key] = k
        loads.append(pltpu.make_async_copy(source, target, load_sem.at[k]))

    def add_down(key, slot, zz, xx):
        add(key, down_ref.at[:, pl.ds(column(zz, xx), half)], wbuf.at[slot])

    for i in range(4):
        add_down(("r", i), i, zdest[i], 1 - x)
    for i in (0, 1):
        add_down(("o", i), 4 + i, zdest[i], x)
    for i in range(8):
        add(("s", i), shrink_ref.at[pl.ds(i * 512, 512), :], sbuf.at[i])
    for i in (3, 2):
        add_down(("o", i), 4 + i, zdest[i], x)
    for i in range(4):
        add(("e", i), expand_ref.at[pl.ds(i * 1024, 1024), :], ebuf.at[i])

    mine = pl.ds(pl.multiple_of(c * rows, rows), rows)
    theirs = pl.ds(pl.multiple_of((1 - c) * rows, rows), rows)
    halves = (mine, theirs)
    hid_local = pltpu.make_async_copy(hidden_ref, hid.at[mine], hid_sem.at[2])
    hid_local.start()
    for k in range(DEPTH):
        loads[k].start()

    def use(key):
        k = keys[key]
        loads[k].wait()
        if k + DEPTH < len(loads):
            loads[k + DEPTH].start()

    barrier = pltpu.get_barrier_semaphore()
    for step in range(1, 8):
        pl.semaphore_signal(barrier, inc=1, device_id=dev(c, (tp + step) % 8), device_id_type=MESH)
    xn = z * 2 + 1 - x
    for t in (tp, xn, near * 2 + x, far * 2 + x):
        pl.semaphore_signal(barrier, inc=1, device_id=dev(1 - c, t), device_id_type=MESH)
    pl.semaphore_wait(barrier, 11)

    pending = []

    def send(src, dst, sems, index, pool, t):
        copy = pltpu.make_async_remote_copy(
            src_ref=src, dst_ref=dst,
            send_sem=sems.at[(0, *index)], recv_sem=sems.at[(1, *index)],
            device_id=dev(pool, t), device_id_type=MESH,
        )
        copy.start()
        pending.append(copy)
        return copy

    hid_swap = pltpu.make_async_remote_copy(
        src_ref=hidden_ref, dst_ref=hid.at[mine],
        send_sem=hid_sem.at[0], recv_sem=hid_sem.at[1],
        device_id=dev(1 - c, tp), device_id_type=MESH,
    )
    hid_swap.start()
    x_copies = {}

    def send_x(i, h):
        if i < 3:
            pool, target = c, xr.at[i, halves[h]]
        else:
            pool, target = (c, 1 - c)[h], last.at[0, h]
        x_copies[i, h] = send(xs.at[i, halves[h]], target, x_sem, (2 * i + h,), pool, xn)

    hid_local.wait()
    use(("r", 0))
    for h in range(2):
        if h == 1:
            hid_swap.wait()
        xs[0, halves[h]] = jnp.dot(
            hid[halves[h], :], wbuf[0], preferred_element_type=f32
        ).astype(bf16)
        send_x(0, h)
    for i in range(1, 4):
        use(("r", i))
        xs[i] = jnp.dot(hid[...], wbuf[i], preferred_element_type=f32).astype(bf16)
        for h in range(2):
            send_x(i, h)

    def own_piece(i):
        use(("o", i))
        own[i] = jnp.dot(hid[...], wbuf[4 + i], preferred_element_type=f32)

    z_copies = {}

    def forward(i):
        for h in range(2):
            part = halves[h]
            x_copies[i, h].wait_recv()
            total = own[i, part] + xr[i, part].astype(f32)
            if i == 1:
                z_copies[0, h].wait_recv()
                total = total + pair[part, :].astype(f32)
            zs[i, part] = total.astype(bf16)
            if i == 0:
                pool, target = c, pair.at[part]
            else:
                pool, target = (c, 1 - c)[h], last.at[i, h]
            z_copies[i, h] = send(
                zs.at[i, part], target, z_sem, (i, h), pool, (far if i == 1 else near) * 2 + x
            )

    own_piece(0)
    own_piece(1)

    pids = []
    for s in range(2):
        slot = jnp.transpose(jnp.broadcast_to(slots_ref[s : s + 1, :], (rows, rows)))
        adapter = jnp.sum(
            jnp.where(lane((rows, 32)) == slot[:, :32], requests_ref[s : s + 1, :], 0),
            axis=1, keepdims=True,
        )
        pids.append(
            jnp.sum(
                jnp.where(lane((rows, 128)) == adapter, table_ref[...], 0), axis=1, keepdims=True
            )
        )
    pid = jnp.concatenate(pids, axis=0) - c * 64
    pid2 = jnp.broadcast_to(pid, (2 * rows, 128)) - lane((2 * rows, 128)) // 64

    acc = jnp.zeros((2 * rows, 128), f32)
    for i in range(8):
        use(("s", i))
        scores = lax.dot_general(
            hid[...], sbuf[i], (((1,), (1,)), ((), ())), preferred_element_type=f32
        )
        for j in range(4):
            acc = acc + jnp.where(pid2 == 8 * i + 2 * j, scores[:, j * 128 : j * 128 + 128], 0.0)
        if i == SPLIT:
            forward(0)
    acc = acc + pltpu.roll(acc, 64, 1)
    low = lane((rows, 128)) < 64
    pack[...] = jnp.where(low, acc[:rows], acc[rows:])
    l_copies = []
    for step in range(1, 8):
        to = (tp + step) % 8
        source = pack.at[pl.ds(pl.multiple_of(to * 16, 16), 16)]
        l_copies.append(send(source, lrr.at[step - 1], l_sem, (step - 1,), c, to))

    own_piece(3)
    bs[...] = own[3, theirs, :]
    b_copy = send(bs, br, b_sem, (), 1 - c, tp)
    own_piece(2)
    forward(1)

    block = pl.ds(pl.multiple_of(tp * 16, 16), 16)
    total = pack[block, :]
    for step in range(1, 8):
        l_copies[step - 1].wait_recv()
        total = total + lrr[step - 1]
    lrs[...] = total.astype(bf16)
    lrg[block, :] = lrs[...]
    g_copies = []
    for step in range(1, 8):
        to = (tp + step) % 8
        g_copies.append(send(lrs, lrg.at[block], g_sem, (step - 1,), c, to))

    forward(2)

    for step in range(1, 8):
        g_copies[step - 1].wait_recv()
    packed = lrg[...].astype(f32)
    turned = pltpu.roll(packed, 64, 1)
    rank2 = jnp.concatenate(
        [jnp.where(low, packed, turned), jnp.where(low, turned, packed)], axis=0
    )
    for i in range(4):
        use(("e", i))
        weighted = jnp.concatenate(
            [jnp.where(pid2 == 16 * i + 2 * j, rank2, 0.0).astype(bf16) for j in range(8)],
            axis=1,
        )
        part = jnp.dot(weighted, ebuf[i], preferred_element_type=f32)
        if i == 0:
            delta[...] = part
        else:
            delta[...] += part
    ds_[...] = delta[theirs, :]
    d_copy = send(ds_, dr, d_sem, (), 1 - c, tp)

    own_cols = pl.ds(pl.multiple_of(c * half, half), half)
    other_cols = pl.ds(pl.multiple_of((1 - c) * half, half), half)
    b_copy.wait_recv()
    d_copy.wait_recv()
    base = [
        own[3, mine, :] + delta[mine, own_cols] + dr[:, own_cols],
        br[...] + delta[mine, other_cols] + dr[:, other_cols],
    ]
    for i, copies in ((1, z_copies), (2, z_copies), (0, x_copies)):
        for h in range(2):
            copies[3 if i == 0 else i, h].wait_recv()
            base[h] = base[h] + last[i, h].astype(f32)
    out_ref[:, own_cols] = base[0].astype(bf16)
    out_ref[:, other_cols] = base[1].astype(bf16)

    for copy in pending:
        copy.wait_send()


def local_fused(
    hidden,
    row_request_slots,
    requests,
    adapter_page_table,
    down_matrix,
    shrink_pool_pages,
    expand_pool_pages,
):
    rows, depth = hidden.shape
    pages, rank, width = expand_pool_pages.shape
    half = width // 2
    bf16, f32 = jnp.bfloat16, jnp.float32
    vmem = pl.BlockSpec(memory_space=pltpu.VMEM)
    hbm = pl.BlockSpec(memory_space=pl.ANY)
    V = pltpu.VMEM
    dma = pltpu.SemaphoreType.DMA
    flat = pages * rank
    return pl.pallas_call(
        fused_kernel,
        out_shape=jax.ShapeDtypeStruct((rows, width), bf16),
        in_specs=[vmem, vmem, vmem, hbm, hbm, hbm, hbm],
        out_specs=vmem,
        scratch_shapes=[
            V((2 * rows, depth), bf16),
            V((8, depth, half), bf16),
            V((8, flat // 8, depth), bf16),
            V((4, flat // 4, width), bf16),
            V((4, 2 * rows, half), f32),
            V((4, 2 * rows, half), bf16),
            V((3, 2 * rows, half), bf16),
            V((3, 2 * rows, half), bf16),
            V((2 * rows, half), bf16),
            V((3, 2, rows, half), bf16),
            V((rows, half), f32),
            V((rows, half), f32),
            V((2 * rows, width), f32),
            V((rows, width), f32),
            V((rows, width), f32),
            V((rows, 128), f32),
            V((7, 16, 128), f32),
            V((16, 128), bf16),
            V((rows, 128), bf16),
            dma((20,)),
            dma((3,)),
            dma((2, 8)),
            dma((2, 3, 2)),
            dma((2,)),
            dma((2,)),
            dma((2, 7)),
            dma((2, 7)),
        ],
        compiler_params=pltpu.CompilerParams(
            collective_id=0, has_side_effects=True, vmem_limit_bytes=60 * 1024 * 1024
        ),
    )(
        row_request_slots.reshape(-1, rows),
        requests,
        adapter_page_table.reshape(1, -1),
        hidden,
        down_matrix,
        shrink_pool_pages.reshape(flat, depth),
        expand_pool_pages.reshape(flat, width),
    )


def solution(mesh):
    return jax.shard_map(
        local_fused if mesh.shape["tp"] == 8 else local_general,
        mesh=mesh,
        in_specs=(
            P(("rep", "pool"), "tp"),
            P("rep"),
            P("rep", None),
            P(),
            P("tp", None),
            P("pool", None, "tp"),
            P("pool", None, "tp"),
        ),
        out_specs=P(("rep", "pool"), "tp"),
        check_vma=False,
    )
```

time: 54.3 us -> 45.2 us (0.83)
  Pallas kernels: 50.8 us -> 43.1 us
  local copies, waits for them, and re-layouts: 3.14 us -> 1.67 us
    pallas_call x1, Pallas kernels: 50.8 us -> 43.1 us  [local_fused(): pl.pallas_call(fused_kernel, out_shape=jax.ShapeDtypeStruct((rows, width)...]
    reshape x1 -> x0, local copies, waits for them, and re-layouts: 1.47 us -> none  [local_fused(): row_request_slots.reshape(-1, 1)]
where the time goes in v2:
time: 45.2 us; the launch traced here: 44.8 us
  Pallas kernels  43.1 us (95%)
  local copies, waits for them, and re-layouts  1.67 us (4%)
    pallas_call x1, Pallas kernels, local_fused(): pl.pallas_call(fused_kernel, out_shape=jax.ShapeDtypeStruct((rows, width)...  43.1 us
    unnamed x1, local copies, waits for them, and re-layouts  1.67 us

profile of v2, /device:TPU:0, one launch (start us, length us, event | category | flops | bytes accessed | tf_op | source)
XLA Modules:
  0.0 44.8 jit_solution(973021244720170895)
XLA Ops:
  0.0 43.1 %shard_map.73 = bf16[128,1024]{1,0:T(8,128)(2,1)} custom-call(s32[2,128]{1,0:T(2,128)} %bitcast.6, s32[2,32]{1,0:T(2,128)} %requests_ref.1, s32[1,128]{1,0:T(1,128)} %bitcast.7, bf16[128,2048]{1,0:T(8,128)(2,1)} %hidden_ref.1, bf16[2048,8192]{1,0:T(8,128)(2,1)} %down_ref.1, bf16[4096,2048]{1,0:T(8,128)(2,1)} %bitcast.4, bf16[4096,1024]{1,0:T(8,128)(2,1)} %bitcast.5), custom_call_target="tpu_custom_call" | custom-call | tf_op jit(solution)/shard_map/pallas_call | solution.py:351
  43.1 1.7 %copy.9 = bf16[128,1024]{1,0:T(8,128)(2,1)} copy(bf16[128,1024]{1,0:T(8,128)(2,1)} %shard_map.73) | data formatting | bytes 524288

commit v3 on v2

--- a/solution.py
+++ b/solution.py
@@ -8,7 +8,7 @@
 from jax.sharding import PartitionSpec as P
 
 MESH = pl.DeviceIdType.MESH
-DEPTH = 6
+DEPTH = 4
 SPLIT = 3
 
 
@@ -207,8 +207,9 @@
     for i in range(1, 4):
         use(("r", i))
         xs[i] = jnp.dot(hid[...], wbuf[i], preferred_element_type=f32).astype(bf16)
-        for h in range(2):
-            send_x(i, h)
+        if i == 1:
+            for h in range(2):
+                send_x(i, h)
 
     def own_piece(i):
         use(("o", i))
@@ -270,11 +271,12 @@
         source = pack.at[pl.ds(pl.multiple_of(to * 16, 16), 16)]
         l_copies.append(send(source, lrr.at[step - 1], l_sem, (step - 1,), c, to))
 
+    for h in range(2):
+        send_x(2, h)
     own_piece(3)
     bs[...] = own[3, theirs, :]
     b_copy = send(bs, br, b_sem, (), 1 - c, tp)
     own_piece(2)
-    forward(1)
 
     block = pl.ds(pl.multiple_of(tp * 16, 16), 16)
     total = pack[block, :]
@@ -288,6 +290,9 @@
         to = (tp + step) % 8
         g_copies.append(send(lrs, lrg.at[block], g_sem, (step - 1,), c, to))
 
+    for h in range(2):
+        send_x(3, h)
+    forward(1)
     forward(2)
 
     for step in range(1, 8):

time: 45.2 us -> 41.2 us (0.912)
  Pallas kernels: 43.1 us -> 39.1 us
    pallas_call x1, Pallas kernels: 43.1 us -> 39.1 us  [local_fused(): pl.pallas_call(fused_kernel, out_shape=jax.ShapeDtypeStruct((rows, width)...]
where the time goes in v3:
time: 41.2 us; the launch traced here: 40.8 us
  Pallas kernels  39.1 us (95%)
  local copies, waits for them, and re-layouts  1.67 us (4%)
    pallas_call x1, Pallas kernels, local_fused(): pl.pallas_call(fused_kernel, out_shape=jax.ShapeDtypeStruct((rows, width)...  39.1 us
    unnamed x1, local copies, waits for them, and re-layouts  1.67 us

profile of v3, /device:TPU:0, one launch (start us, length us, event | category | flops | bytes accessed | tf_op | source)
XLA Modules:
  0.0 40.8 jit_solution(9164797950937445184)
XLA Ops:
  0.0 39.1 %shard_map.73 = bf16[128,1024]{1,0:T(8,128)(2,1)} custom-call(s32[2,128]{1,0:T(2,128)} %bitcast.6, s32[2,32]{1,0:T(2,128)} %requests_ref.1, s32[1,128]{1,0:T(1,128)} %bitcast.7, bf16[128,2048]{1,0:T(8,128)(2,1)} %hidden_ref.1, bf16[2048,8192]{1,0:T(8,128)(2,1)} %down_ref.1, bf16[4096,2048]{1,0:T(8,128)(2,1)} %bitcast.4, bf16[4096,1024]{1,0:T(8,128)(2,1)} %bitcast.5), custom_call_target="tpu_custom_call" | custom-call | tf_op jit(solution)/shard_map/pallas_call | solution.py:356
  39.1 1.7 %copy.9 = bf16[128,1024]{1,0:T(8,128)(2,1)} copy(bf16[128,1024]{1,0:T(8,128)(2,1)} %shard_map.73) | data formatting | bytes 524288
